TPU v7x, 32 devices: a whole 2x2x4 slice. The times are simulated.
32 devices in a mesh: ctx: 8 (over z, x), tp: 4 (over y, core).
Axes of the slice: x: 2, y: 2, z: 4, core: 2. Of those that a mesh axis runs over, the one named last changes fastest.
Arguments:
- projected: bfloat16 [1024, 3, 4096], P('ctx', None, 'tp'), may hold values from -6 to 6
- short_taps: float32 [3, 7, 4096], P(None, None, 'tp'), may hold values from -2 to 2
- residues: float32 [4096, 16], P('tp'), may hold values from -6 to 6
- rates: float32 [4096, 16], P('tp'), may hold values from 0.3 to 64
- skip_gain: float32 [4096], P('tp'), may hold values from -1 to 1
- norm_gain: float32 [4096], P('tp'), may hold values from 0.5 to 1.5
Outputs:
- mixed_out: bfloat16 [1024, 4096], P('ctx', 'tp')
All inputs are finite; a program needn't handle non-finite values.
Results may differ from a plain program's by a relative error of at most 0.008.
Values may be sent and summed in bfloat16 or wider, within the bound.
A program may use at most 64 MiB of HBM per device.

v0:
```python
import functools
import math

import jax
import jax.numpy as jnp
import ml_dtypes
import numpy as np
from jax import lax
from jax.experimental import pallas as pl
from jax.experimental.pallas import tpu as pltpu
from jax.sharding import PartitionSpec as P

LANES = 128
SUB = 8
HIGHEST = lax.Precision.HIGHEST


def tables(rows):
    freq = (np.arange(rows) + 0.5)[:, None] * (2.0 * math.pi / (2 * rows))
    angle = freq * np.arange(rows)[None, :]
    forward = np.concatenate([np.cos(angle), -np.sin(angle)], 0)
    inverse = forward.T / rows

    def pair(a):
        hi = a.astype(ml_dtypes.bfloat16)
        lo = (a - hi.astype(np.float64)).astype(ml_dtypes.bfloat16)
        return hi, lo

    f_hi, f_lo = pair(forward)
    g_hi, g_lo = pair(inverse)
    return np.concatenate([f_hi, f_lo], 1), g_hi, g_lo


def kernel(
    n, m, modes, taps_n, rows, channels, length,
    proj, taps, res, rates, skip, gain, fwd, inv_hi, inv_lo,
    out,
    x, kv, state, state0, filt, tailw, a8, a128, long, gated, squares,
    send_kv, halo_kv, halo_q, end_f, end_b, ends, sums,
    halo_send, halo_recv, end_send, end_recv, sum_send, sum_recv,
):
    me = lax.axis_index("ctx")
    lane_rank = lax.axis_index("tp")
    tiles = channels // LANES
    blocks = rows // SUB
    dot = functools.partial(jnp.dot, preferred_element_type=jnp.float32)

    barrier = pltpu.get_barrier_semaphore()

    def greet(i, _):
        pl.semaphore_signal(barrier, inc=1, device_id={"ctx": i}, device_id_type=pl.DeviceIdType.MESH)
        return 0

    lax.fori_loop(0, me, greet, 0)
    for d in range(1, m):
        pl.semaphore_signal(
            barrier, inc=1, device_id={"tp": lax.rem(lane_rank + d, m)}, device_id_type=pl.DeviceIdType.MESH
        )

    rim_k = proj[1, rows - 16 :, :].astype(jnp.float32)[SUB:]
    rim_v = proj[2, rows - 16 :, :].astype(jnp.float32)[SUB:]
    send_kv[...] = jnp.concatenate([rim_k, rim_v], 0).astype(jnp.bfloat16)
    pl.semaphore_wait(barrier, n - 1 - me + m - 1)

    def halo_copies():
        right = lax.rem(me + 1, n)
        first = pltpu.make_async_remote_copy(
            src_ref=send_kv, dst_ref=halo_kv, send_sem=halo_send.at[0], recv_sem=halo_recv.at[0],
            device_id={"ctx": right}, device_id_type=pl.DeviceIdType.MESH,
        )
        second = pltpu.make_async_remote_copy(
            src_ref=proj.at[0, pl.ds(rows - 16, 16)], dst_ref=halo_q, send_sem=halo_send.at[1],
            recv_sem=halo_recv.at[1], device_id={"ctx": right}, device_id_type=pl.DeviceIdType.MESH,
        )
        return first, second

    @pl.when(me < n - 1)
    def _():
        first, second = halo_copies()
        first.start()
        second.start()

    sub = lax.broadcasted_iota(jnp.int32, (SUB, LANES), 0).astype(jnp.float32)
    scale = 1.0 / math.sqrt(length)
    rate_all = rates[...]
    a8[...] = jnp.exp(-(rate_all * SUB) / length)
    a128[...] = jnp.exp(-(rate_all * rows) / length)

    def columns(t):
        return pl.ds(pl.multiple_of(t * LANES, LANES), LANES)

    def short(g, t, start, count):
        cols = columns(t)
        total = None
        for j in range(taps_n):
            term = taps[g, j : j + 1, cols] * x[g, t, pl.ds(SUB + start - j, count), :]
            total = term if total is None else total + term
        return total

    def rounded(a):
        return a.astype(jnp.bfloat16).astype(jnp.float32)

    def body_a(t, _):
        cols = columns(t)
        for g in range(3):
            x[g, t, pl.ds(SUB, rows), :] = proj[g, :, cols].astype(jnp.float32)
        kv[t, pl.ds(SUB, rows - SUB), :] = rounded(
            short(1, t, SUB, rows - SUB) * short(2, t, SUB, rows - SUB)
        )
        step = [jnp.broadcast_to(a8[i : i + 1, cols], (SUB, LANES)) for i in range(modes)]
        s = [kv[t, pl.ds(SUB, SUB), :]] * modes
        for b in range(2, blocks):
            u = kv[t, pl.ds(b * SUB, SUB), :]
            s = [step[i] * s[i] + u for i in range(modes)]
        for i in range(modes):
            r = rates[i : i + 1, cols]
            state[i, t] = s[i] * jnp.exp(-(r * (SUB - 1 - sub)) / length)
            state0[i, t] = jnp.exp(-(r * (rows - 1 - sub)) / length)
        return 0

    lax.fori_loop(0, tiles, body_a, 0)

    @pl.when(me > 0)
    def _():
        first, _second = halo_copies()
        first.wait_recv()
        rim = halo_kv[...].astype(jnp.float32)
        for t in range(tiles):
            x[1, t, pl.ds(0, SUB), :] = rim[:SUB, t * LANES : (t + 1) * LANES]
            x[2, t, pl.ds(0, SUB), :] = rim[SUB:, t * LANES : (t + 1) * LANES]

    @pl.when(me == 0)
    def _():
        for g in range(3):
            for t in range(tiles):
                x[g, t, pl.ds(0, SUB), :] = jnp.zeros((SUB, LANES), jnp.float32)

    def body_b(t, _):
        cols = columns(t)
        u = rounded(short(1, t, 0, SUB) * short(2, t, 0, SUB))
        kv[t, pl.ds(0, SUB), :] = u
        for i in range(modes):
            end_f[i : i + 1, cols] = jnp.sum(state[i, t] + state0[i, t] * u, axis=0, keepdims=True)
        return 0

    lax.fori_loop(0, tiles, body_b, 0)
    end_b[...] = end_f[...].astype(jnp.bfloat16)

    def end_copy(slot, target):
        return pltpu.make_async_remote_copy(
            src_ref=end_b, dst_ref=ends.at[slot], send_sem=end_send.at[target], recv_sem=end_recv.at[slot],
            device_id={"ctx": target}, device_id_type=pl.DeviceIdType.MESH,
        )

    def send_end(j, _):
        end_copy(me, j).start()
        return 0

    lax.fori_loop(me + 1, n, send_end, 0)

    def body_c(t, _):
        cols = columns(t)
        step = [jnp.broadcast_to(a8[i : i + 1, cols], (SUB, LANES)) for i in range(modes)]
        w = []
        for i in range(modes):
            r = rates[i : i + 1, cols]
            c = res[i : i + 1, cols] * scale
            w.append(c * jnp.exp(-(r * sub) / length))
            tailw[i, t] = c * jnp.exp(-(r * (sub + 1.0)) / length)
        for b in range(blocks):
            total = w[0]
            for i in range(1, modes):
                total = total + w[i]
            filt[t, pl.ds(b * SUB, SUB), :] = total
            if b < blocks - 1:
                w = [w[i] * step[i] for i in range(modes)]
        return 0

    lax.fori_loop(0, tiles, body_c, 0)

    def body_d(p, _):
        t0 = 2 * p
        u = jnp.concatenate([kv[t0], kv[t0 + 1]], 1).astype(jnp.bfloat16)
        f = jnp.concatenate([filt[t0], filt[t0 + 1]], 1)
        f_hi = f.astype(jnp.bfloat16)
        f_lo = (f - f_hi.astype(jnp.float32)).astype(jnp.bfloat16)
        both = fwd[...]
        us = dot(both, jnp.concatenate([u, u], 0))
        fs = dot(both, jnp.concatenate([f_hi, f_hi], 0)) + dot(both[:, :rows], f_lo)
        ur, ui, fr, fi = us[:rows], us[rows:], fs[:rows], fs[rows:]
        prod = jnp.concatenate([ur * fr - ui * fi, ur * fi + ui * fr], 0)
        p_hi = prod.astype(jnp.bfloat16)
        p_lo = (prod - p_hi.astype(jnp.float32)).astype(jnp.bfloat16)
        y = dot(inv_hi[...], p_hi) + dot(inv_lo[...], p_hi) + dot(inv_hi[...], p_lo)
        long[t0] = y[:, :LANES]
        long[t0 + 1] = y[:, LANES:]
        return 0

    lax.fori_loop(0, tiles // 2, body_d, 0)

    @pl.when(me > 0)
    def _():
        _first, second = halo_copies()
        second.wait_recv()
        rim = halo_q[...].astype(jnp.float32)[SUB:]
        for t in range(tiles):
            x[0, t, pl.ds(0, SUB), :] = rim[:, t * LANES : (t + 1) * LANES]

    def body_q(t, _):
        gated[t] = short(0, t, 0, rows)
        return 0

    lax.fori_loop(0, tiles, body_q, 0)

    def gather(i, carry):
        end_copy(i, i).wait_recv()
        return carry * a128[...] + ends[i].astype(jnp.float32)

    end_f[...] = lax.fori_loop(0, me, gather, jnp.zeros((modes, channels), jnp.float32))
    squares[...] = jnp.zeros_like(squares)

    def body_e(t, _):
        cols = columns(t)
        step = [jnp.broadcast_to(a8[i : i + 1, cols], (SUB, LANES)) for i in range(modes)]
        w = [tailw[i, t] * end_f[i : i + 1, cols] for i in range(modes)]
        direct = skip[:, cols]
        for b in range(blocks):
            here = pl.ds(b * SUB, SUB)
            total = w[0]
            for i in range(1, modes):
                total = total + w[i]
            y = rounded(long[t, here, :] + total)
            g = gated[t, here, :] * (y + direct * kv[t, here, :])
            gated[t, here, :] = g
            squares[here, :] += g * g
            if b < blocks - 1:
                w = [w[i] * step[i] for i in range(modes)]
        return 0

    lax.fori_loop(0, tiles, body_e, 0)

    ones = jnp.ones((SUB, LANES), jnp.float32)
    mine = lax.dot_general(
        ones, squares[...], (((1,), (1,)), ((), ())), precision=HIGHEST, preferred_element_type=jnp.float32
    )
    sums[lane_rank] = mine

    def sum_copy(d, slot):
        return pltpu.make_async_remote_copy(
            src_ref=sums.at[lane_rank], dst_ref=sums.at[slot], send_sem=sum_send.at[d],
            recv_sem=sum_recv.at[slot], device_id={"tp": lax.rem(lane_rank + d, m)},
            device_id_type=pl.DeviceIdType.MESH,
        )

    for d in range(1, m):
        sum_copy(d, lane_rank).start()
    for d in range(1, m):
        sum_copy(d, lax.rem(lane_rank + d, m)).wait_recv()
    total = sums[0]
    for d in range(1, m):
        total = total + sums[d]
    inverse = 1.0 / jnp.sqrt(total / (channels * m) + 1e-05)
    spread = lax.dot_general(
        inverse, ones * (1.0 / SUB), (((0,), (0,)), ((), ())), precision=HIGHEST,
        preferred_element_type=jnp.float32,
    )

    for t in range(tiles):
        cols = slice(t * LANES, (t + 1) * LANES)
        out[:, cols] = (gated[t] * gain[:, cols] * spread).astype(jnp.bfloat16)

    @pl.when(me < n - 1)
    def _():
        first, second = halo_copies()
        first.wait_send()
        second.wait_send()

    def finish(j, _):
        end_copy(me, j).wait_send()
        return 0

    lax.fori_loop(me + 1, n, finish, 0)
    for d in range(1, m):
        sum_copy(d, lane_rank).wait_send()


def solution(mesh):
    n, m = mesh.shape["ctx"], mesh.shape["tp"]

    def shards(projected, short_taps, residues, rates, skip_gain, norm_gain):
        rows, _, channels = projected.shape
        modes = rates.shape[1]
        tiles = channels // LANES
        f32, bf16 = jnp.float32, jnp.bfloat16
        fwd, inv_hi, inv_lo = (jnp.asarray(a) for a in tables(rows))
        tile3 = pltpu.VMEM((tiles, rows, LANES), f32)
        modal = pltpu.VMEM((modes, tiles, SUB, LANES), f32)
        flat = pltpu.VMEM((modes, channels), f32)
        dma = pltpu.SemaphoreType.DMA
        return pl.pallas_call(
            functools.partial(kernel, n, m, modes, short_taps.shape[1], rows, channels, rows * n),
            out_shape=jax.ShapeDtypeStruct((rows, channels), bf16),
            in_specs=[pl.BlockSpec(memory_space=pltpu.VMEM)] * 9,
            out_specs=pl.BlockSpec(memory_space=pltpu.VMEM),
            scratch_shapes=[
                pltpu.VMEM((3, tiles, rows + SUB, LANES), f32),
                tile3, modal, modal, tile3, modal, flat, flat, tile3, tile3,
                pltpu.VMEM((rows, LANES), f32),
                pltpu.VMEM((16, channels), bf16),
                pltpu.VMEM((16, channels), bf16),
                pltpu.VMEM((16, channels), bf16),
                flat,
                pltpu.VMEM((modes, channels), bf16),
                pltpu.VMEM((n, modes, channels), bf16),
                pltpu.VMEM((m, SUB, LANES), f32),
                dma((2,)), dma((2,)), dma((n,)), dma((n,)), dma((m,)), dma((m,)),
            ],
            compiler_params=pltpu.CompilerParams(
                collective_id=0, has_side_effects=True, vmem_limit_bytes=32 * 1024 * 1024
            ),
        )(
            jnp.transpose(projected, (1, 0, 2)), short_taps, residues.T, rates.T,
            skip_gain[None, :], norm_gain[None, :], fwd, inv_hi, inv_lo,
        )

    return jax.shard_map(
        shards,
        mesh=mesh,
        in_specs=(
            P("ctx", None, "tp"),
            P(None, None, "tp"),
            P("tp", None),
            P("tp", None),
            P("tp"),
            P("tp"),
        ),
        out_specs=P("ctx", "tp"),
        check_vma=False,
    )
```

profile of v0, /device:TPU:27, one launch (start us, length us, event | category | flops | bytes accessed | tf_op | source)
XLA Modules:
  0.0 25.5 jit_solution(8848993855499210800)
XLA Ops:
  0.0 0.0 copy-start.8
  0.0 0.0 copy-start.7
  0.0 0.7 %copy-done.8 = f32[1024]{0:T(1024)S(1)} copy-done((f32[1024]{0:T(1024)S(1)}, f32[1024]{0:T(1024)}, u32[]{:S(2)}) %copy-start.8) | copy-done | bytes 4120
  0.7 0.0 copy-done.7
  0.7 0.0 copy-start
  0.7 1.1 %copy-done = bf16[128,3,1024]{2,0,1:T(8,128)(2,1)S(1)} copy-done((bf16[128,3,1024]{2,0,1:T(8,128)(2,1)S(1)}, bf16[128,3,1024]{2,0,1:T(8,128)(2,1)}, u32[]{:S(2)}) %copy-start) | copy-done | bytes 786456
  1.8 0.0 copy-start.1
  1.8 0.9 %copy-done.1 = bf16[256,256]{1,0:T(8,128)(2,1)S(1)} copy-done((bf16[256,256]{1,0:T(8,128)(2,1)S(1)}, bf16[256,256]{1,0:T(8,128)(2,1)}, u32[]{:S(2)}) %copy-start.1) | copy-done | bytes 131096
  2.7 0.0 copy-start.2
  2.7 0.9 %copy-done.2 = f32[3,7,1024]{2,1,0:T(8,128)S(1)} copy-done((f32[3,7,1024]{2,1,0:T(8,128)S(1)}, f32[3,7,1024]{2,1,0:T(8,128)}, u32[]{:S(2)}) %copy-start.2) | copy-done | bytes 86040
  3.6 0.0 copy-start.3
  3.6 0.8 %copy-done.3 = f32[1024,16]{0,1:T(8,128)S(1)} copy-done((f32[1024,16]{0,1:T(8,128)S(1)}, f32[1024,16]{0,1:T(8,128)}, u32[]{:S(2)}) %copy-start.3) | copy-done | bytes 65560
  4.5 0.0 copy-start.4
  4.5 0.8 %copy-done.4 = f32[1024,16]{0,1:T(8,128)S(1)} copy-done((f32[1024,16]{0,1:T(8,128)S(1)}, f32[1024,16]{0,1:T(8,128)}, u32[]{:S(2)}) %copy-start.4) | copy-done | bytes 65560
  5.3 0.0 copy-start.5
  5.3 0.8 %copy-done.5 = bf16[128,256]{1,0:T(8,128)(2,1)S(1)} copy-done((bf16[128,256]{1,0:T(8,128)(2,1)S(1)}, bf16[128,256]{1,0:T(8,128)(2,1)}, u32[]{:S(2)}) %copy-start.5) | copy-done | bytes 65560
  6.2 0.0 copy-start.6
  6.2 0.8 %copy-done.6 = bf16[128,256]{1,0:T(8,128)(2,1)S(1)} copy-done((bf16[128,256]{1,0:T(8,128)(2,1)S(1)}, bf16[128,256]{1,0:T(8,128)(2,1)}, u32[]{:S(2)}) %copy-start.6) | copy-done | bytes 65560
  7.0 17.8 %shard_map.91 = bf16[128,1024]{1,0:T(8,128)(2,1)S(1)} custom-call(bf16[3,128,1024]{2,1,0:T(8,128)(2,1)S(1)} %bitcast.5, f32[3,7,1024]{2,1,0:T(8,128)S(1)} %copy-done.2, f32[16,1024]{1,0:T(8,128)S(1)} %bitcast.6, f32[16,1024]{1,0:T(8,128)S(1)} %bitcast.7, f32[1,1024]{1,0:T(1,128)S(1)} %bitcast.8, f32[1,1024]{1,0:T(1,128)S(1)} %bitcast.9, ...), custom_call_target="tpu_custom_call" | custom-call | tf_op jit(solution)/shard_map/pallas_call | solution.py:300
  24.8 0.7 %copy.11 = bf16[128,1024]{1,0:T(8,128)(2,1)} copy(bf16[128,1024]{1,0:T(8,128)(2,1)S(1)} %shard_map.91) | data formatting | bytes 524288
Async XLA Ops:
  0.0 0.7 %copy-start.8 = (f32[1024]{0:T(1024)S(1)}, f32[1024]{0:T(1024)}, u32[]{:S(2)}) copy-start(f32[1024]{0:T(1024)} %param.14) | copy-start | bytes 12292
  0.0 0.7 %copy-start.7 = (f32[1024]{0:T(1024)S(1)}, f32[1024]{0:T(1024)}, u32[]{:S(2)}) copy-start(f32[1024]{0:T(1024)} %param.13) | copy-start | bytes 12292
  0.7 1.1 %copy-start = (bf16[128,3,1024]{2,0,1:T(8,128)(2,1)S(1)}, bf16[128,3,1024]{2,0,1:T(8,128)(2,1)}, u32[]{:S(2)}) copy-start(bf16[128,3,1024]{2,0,1:T(8,128)(2,1)} %param.9) | copy-start | bytes 2359300
  1.8 0.9 %copy-start.1 = (bf16[256,256]{1,0:T(8,128)(2,1)S(1)}, bf16[256,256]{1,0:T(8,128)(2,1)}, u32[]{:S(2)}) copy-start(bf16[256,256]{1,0:T(8,128)(2,1)} %constant.6.clone.fwd) | copy-start | bytes 393220
  2.7 0.9 %copy-start.2 = (f32[3,7,1024]{2,1,0:T(8,128)S(1)}, f32[3,7,1024]{2,1,0:T(8,128)}, u32[]{:S(2)}) copy-start(f32[3,7,1024]{2,1,0:T(8,128)} %taps.1) | copy-start | bytes 258052
  3.6 0.8 %copy-start.3 = (f32[1024,16]{0,1:T(8,128)S(1)}, f32[1024,16]{0,1:T(8,128)}, u32[]{:S(2)}) copy-start(f32[1024,16]{0,1:T(8,128)} %param.11) | copy-start | bytes 196612
  4.5 0.8 %copy-start.4 = (f32[1024,16]{0,1:T(8,128)S(1)}, f32[1024,16]{0,1:T(8,128)}, u32[]{:S(2)}) copy-start(f32[1024,16]{0,1:T(8,128)} %param.12) | copy-start | bytes 196612
  5.3 0.8 %copy-start.5 = (bf16[128,256]{1,0:T(8,128)(2,1)S(1)}, bf16[128,256]{1,0:T(8,128)(2,1)}, u32[]{:S(2)}) copy-start(bf16[128,256]{1,0:T(8,128)(2,1)} %constant.8.clone.inv_lo) | copy-start | bytes 196612
  6.2 0.8 %copy-start.6 = (bf16[128,256]{1,0:T(8,128)(2,1)S(1)}, bf16[128,256]{1,0:T(8,128)(2,1)}, u32[]{:S(2)}) copy-start(bf16[128,256]{1,0:T(8,128)(2,1)} %constant.7.clone.inv_hi) | copy-start | bytes 196612
where the time goes:
time: 25.9 us; the launch traced here: 25.5 us
  Pallas kernels  17.8 us (69%)
  local copies, waits for them, and re-layouts  7.69 us (30%)
    pallas_call x1, Pallas kernels, shards(): pl.pallas_call(functools.partial(kernel, n, m, modes, short_taps.shape[1]...  17.8 us
    unnamed x19, local copies, waits for them, and re-layouts  7.69 us

commit v1 on v0

--- a/solution.py
+++ b/solution.py
@@ -33,8 +33,9 @@
 
 def kernel(
     n, m, modes, taps_n, rows, channels, length,
-    proj, taps, res, rates, skip, gain, fwd, inv_hi, inv_lo,
+    proj_h, taps_h, res_h, rates_h, skip_h, gain_h, fwd_h, inv_hi_h, inv_lo_h,
     out,
+    rim, proj, taps, res, rates, skip, gain, fwd, inv_hi, inv_lo, load_sem,
     x, kv, state, state0, filt, tailw, a8, a128, long, gated, squares,
     send_kv, halo_kv, halo_q, end_f, end_b, ends, sums,
     halo_send, halo_recv, end_send, end_recv, sum_send, sum_recv,
@@ -45,6 +46,17 @@
     blocks = rows // SUB
     dot = functools.partial(jnp.dot, preferred_element_type=jnp.float32)
 
+    pairs = [
+        (proj_h.at[pl.ds(1, 2), pl.ds(rows - 16, 16)], rim),
+        (proj_h.at[pl.ds(1, 2)], proj.at[pl.ds(1, 2)]),
+        (taps_h, taps), (rates_h, rates), (res_h, res),
+        (proj_h.at[0], proj.at[0]),
+        (fwd_h, fwd), (inv_hi_h, inv_hi), (inv_lo_h, inv_lo), (skip_h, skip), (gain_h, gain),
+    ]
+    loads = [pltpu.make_async_copy(a, b, load_sem.at[i]) for i, (a, b) in enumerate(pairs)]
+    for load in loads:
+        load.start()
+
     barrier = pltpu.get_barrier_semaphore()
 
     def greet(i, _):
@@ -57,8 +69,9 @@
             barrier, inc=1, device_id={"tp": lax.rem(lane_rank + d, m)}, device_id_type=pl.DeviceIdType.MESH
         )
 
-    rim_k = proj[1, rows - 16 :, :].astype(jnp.float32)[SUB:]
-    rim_v = proj[2, rows - 16 :, :].astype(jnp.float32)[SUB:]
+    loads[0].wait()
+    rim_k = rim[0].astype(jnp.float32)[SUB:]
+    rim_v = rim[1].astype(jnp.float32)[SUB:]
     send_kv[...] = jnp.concatenate([rim_k, rim_v], 0).astype(jnp.bfloat16)
     pl.semaphore_wait(barrier, n - 1 - me + m - 1)
 
@@ -69,7 +82,7 @@
             device_id={"ctx": right}, device_id_type=pl.DeviceIdType.MESH,
         )
         second = pltpu.make_async_remote_copy(
-            src_ref=proj.at[0, pl.ds(rows - 16, 16)], dst_ref=halo_q, send_sem=halo_send.at[1],
+            src_ref=proj_h.at[0, pl.ds(rows - 16, 16)], dst_ref=halo_q, send_sem=halo_send.at[1],
             recv_sem=halo_recv.at[1], device_id={"ctx": right}, device_id_type=pl.DeviceIdType.MESH,
         )
         return first, second
@@ -82,6 +95,8 @@
 
     sub = lax.broadcasted_iota(jnp.int32, (SUB, LANES), 0).astype(jnp.float32)
     scale = 1.0 / math.sqrt(length)
+    for i in (1, 2, 3):
+        loads[i].wait()
     rate_all = rates[...]
     a8[...] = jnp.exp(-(rate_all * SUB) / length)
     a128[...] = jnp.exp(-(rate_all * rows) / length)
@@ -102,7 +117,7 @@
 
     def body_a(t, _):
         cols = columns(t)
-        for g in range(3):
+        for g in (1, 2):
             x[g, t, pl.ds(SUB, rows), :] = proj[g, :, cols].astype(jnp.float32)
         kv[t, pl.ds(SUB, rows - SUB), :] = rounded(
             short(1, t, SUB, rows - SUB) * short(2, t, SUB, rows - SUB)
@@ -124,10 +139,10 @@
     def _():
         first, _second = halo_copies()
         first.wait_recv()
-        rim = halo_kv[...].astype(jnp.float32)
+        tail = halo_kv[...].astype(jnp.float32)
         for t in range(tiles):
-            x[1, t, pl.ds(0, SUB), :] = rim[:SUB, t * LANES : (t + 1) * LANES]
-            x[2, t, pl.ds(0, SUB), :] = rim[SUB:, t * LANES : (t + 1) * LANES]
+            x[1, t, pl.ds(0, SUB), :] = tail[:SUB, t * LANES : (t + 1) * LANES]
+            x[2, t, pl.ds(0, SUB), :] = tail[SUB:, t * LANES : (t + 1) * LANES]
 
     @pl.when(me == 0)
     def _():
@@ -157,6 +172,8 @@
         return 0
 
     lax.fori_loop(me + 1, n, send_end, 0)
+
+    loads[4].wait()
 
     def body_c(t, _):
         cols = columns(t)
@@ -177,6 +194,9 @@
         return 0
 
     lax.fori_loop(0, tiles, body_c, 0)
+
+    for i in range(5, len(loads)):
+        loads[i].wait()
 
     def body_d(p, _):
         t0 = 2 * p
@@ -202,11 +222,12 @@
     def _():
         _first, second = halo_copies()
         second.wait_recv()
-        rim = halo_q[...].astype(jnp.float32)[SUB:]
+        tail = halo_q[...].astype(jnp.float32)[SUB:]
         for t in range(tiles):
-            x[0, t, pl.ds(0, SUB), :] = rim[:, t * LANES : (t + 1) * LANES]
+            x[0, t, pl.ds(0, SUB), :] = tail[:, t * LANES : (t + 1) * LANES]
 
     def body_q(t, _):
+        x[0, t, pl.ds(SUB, rows), :] = proj[0, :, columns(t)].astype(jnp.float32)
         gated[t] = short(0, t, 0, rows)
         return 0
 
@@ -300,9 +321,15 @@
         return pl.pallas_call(
             functools.partial(kernel, n, m, modes, short_taps.shape[1], rows, channels, rows * n),
             out_shape=jax.ShapeDtypeStruct((rows, channels), bf16),
-            in_specs=[pl.BlockSpec(memory_space=pltpu.VMEM)] * 9,
+            in_specs=[pl.BlockSpec(memory_space=pltpu.HBM)] * 9,
             out_specs=pl.BlockSpec(memory_space=pltpu.VMEM),
             scratch_shapes=[
+                pltpu.VMEM((2, 16, channels), bf16),
+                pltpu.VMEM(projected.shape[1:2] + (rows, channels), bf16),
+                pltpu.VMEM(short_taps.shape, f32), flat, flat,
+                pltpu.VMEM((1, channels), f32), pltpu.VMEM((1, channels), f32),
+                pltpu.VMEM(fwd.shape, bf16), pltpu.VMEM(inv_hi.shape, bf16), pltpu.VMEM(inv_lo.shape, bf16),
+                dma((11,)),
                 pltpu.VMEM((3, tiles, rows + SUB, LANES), f32),
                 tile3, modal, modal, tile3, modal, flat, flat, tile3, tile3,
                 pltpu.VMEM((rows, LANES), f32),
@@ -316,7 +343,7 @@
                 dma((2,)), dma((2,)), dma((n,)), dma((n,)), dma((m,)), dma((m,)),
             ],
             compiler_params=pltpu.CompilerParams(
-                collective_id=0, has_side_effects=True, vmem_limit_bytes=32 * 1024 * 1024
+                collective_id=0, has_side_effects=True, vmem_limit_bytes=60 * 1024 * 1024
             ),
         )(
             jnp.transpose(projected, (1, 0, 2)), short_taps, residues.T, rates.T,

time: 25.9 us -> 20.5 us (0.79)
  the two profiles are of different devices: /device:TPU:27 before, /device:TPU:25 now
where the time goes in v1:
time: 20.5 us; the launch traced here: 20.1 us
  Pallas kernels  18.5 us (90%)
  local copies, waits for them, and re-layouts  1.67 us (8%)
    pallas_call x1, Pallas kernels, shards(): pl.pallas_call(functools.partial(kernel, n, m, modes, short_taps.shape[1]...  18.5 us
    unnamed x1, local copies, waits for them, and re-layouts  1.67 us

profile of v1, /device:TPU:25, one launch (start us, length us, event | category | flops | bytes accessed | tf_op | source)
XLA Modules:
  0.0 20.1 jit_solution(12160498357828318636)
XLA Ops:
  0.0 18.5 %shard_map.91 = bf16[128,1024]{1,0:T(8,128)(2,1)} custom-call(bf16[3,128,1024]{2,1,0:T(8,128)(2,1)} %bitcast.5, f32[3,7,1024]{2,1,0:T(8,128)} %taps_h.1, f32[16,1024]{1,0:T(8,128)} %bitcast.6, f32[16,1024]{1,0:T(8,128)} %bitcast.7, f32[1,1024]{1,0:T(1,128)} %bitcast.8, f32[1,1024]{1,0:T(1,128)} %bitcast.9, bf16[256,256]{1,0:T(8,128)(2,1)} %constant.6.clone.fwd_h, ...), custom_call_target="tpu_custom_call" | custom-call | tf_op jit(solution)/shard_map/pallas_call | solution.py:321
  18.5 1.7 %copy.11 = bf16[128,1024]{1,0:T(8,128)(2,1)} copy(bf16[128,1024]{1,0:T(8,128)(2,1)} %shard_map.91) | data formatting | bytes 524288

commit v2 on v1

--- a/solution.py
+++ b/solution.py
@@ -12,7 +12,6 @@
 
 LANES = 128
 SUB = 8
-HIGHEST = lax.Precision.HIGHEST
 
 
 def tables(rows):
@@ -28,17 +27,17 @@
 
     f_hi, f_lo = pair(forward)
     g_hi, g_lo = pair(inverse)
-    return np.concatenate([f_hi, f_lo], 1), g_hi, g_lo
+    return np.concatenate([f_hi, f_lo, f_hi], 1), np.concatenate([g_hi, g_lo], 0)
 
 
 def kernel(
     n, m, modes, taps_n, rows, channels, length,
-    proj_h, taps_h, res_h, rates_h, skip_h, gain_h, fwd_h, inv_hi_h, inv_lo_h,
+    proj_h, taps_h, res_h, rates_h, skip_h, gain_h, fwd_h, inv_h,
     out,
-    rim, proj, taps, res, rates, skip, gain, fwd, inv_hi, inv_lo, load_sem,
-    x, kv, state, state0, filt, tailw, a8, a128, long, gated, squares,
-    send_kv, halo_kv, halo_q, end_f, end_b, ends, sums,
-    halo_send, halo_recv, end_send, end_recv, sum_send, sum_recv,
+    rim, proj, taps, res, rates, skip, gain, fwd, inv, load_sem,
+    x, kv, state, state0, filt, spec_f, spec_u, prod_hi, prod_lo, tailw, a8, a128, long, gated, squares,
+    send_kv, halo_kv, halo_q, end_f, end_b, mate_b, pair_b, ends, sums,
+    halo_send, halo_recv, end_send, end_recv, sum_send, sum_recv, mate_sem,
 ):
     me = lax.axis_index("ctx")
     lane_rank = lax.axis_index("tp")
@@ -51,7 +50,7 @@
         (proj_h.at[pl.ds(1, 2)], proj.at[pl.ds(1, 2)]),
         (taps_h, taps), (rates_h, rates), (res_h, res),
         (proj_h.at[0], proj.at[0]),
-        (fwd_h, fwd), (inv_hi_h, inv_hi), (inv_lo_h, inv_lo), (skip_h, skip), (gain_h, gain),
+        (fwd_h, fwd), (inv_h, inv), (skip_h, skip), (gain_h, gain),
     ]
     loads = [pltpu.make_async_copy(a, b, load_sem.at[i]) for i, (a, b) in enumerate(pairs)]
     for load in loads:
@@ -59,11 +58,22 @@
 
     barrier = pltpu.get_barrier_semaphore()
 
-    def greet(i, _):
-        pl.semaphore_signal(barrier, inc=1, device_id={"ctx": i}, device_id_type=pl.DeviceIdType.MESH)
-        return 0
-
-    lax.fori_loop(0, me, greet, 0)
+    def greet(target):
+        pl.semaphore_signal(barrier, inc=1, device_id={"ctx": target}, device_id_type=pl.DeviceIdType.MESH)
+
+    pair, side = lax.div(me, 2), lax.rem(me, 2)
+
+    @pl.when(me > 0)
+    def _():
+        greet(me - 1)
+
+    greet(me + 1 - 2 * side)
+
+    def greet_like(i, _):
+        greet(2 * i + side)
+        return 0
+
+    lax.fori_loop(0, pair, greet_like, 0)
     for d in range(1, m):
         pl.semaphore_signal(
             barrier, inc=1, device_id={"tp": lax.rem(lane_rank + d, m)}, device_id_type=pl.DeviceIdType.MESH
@@ -73,7 +83,7 @@
     rim_k = rim[0].astype(jnp.float32)[SUB:]
     rim_v = rim[1].astype(jnp.float32)[SUB:]
     send_kv[...] = jnp.concatenate([rim_k, rim_v], 0).astype(jnp.bfloat16)
-    pl.semaphore_wait(barrier, n - 1 - me + m - 1)
+    pl.semaphore_wait(barrier, jnp.where(me < n - 1, 1, 0) + 1 + (n // 2 - 1 - pair) + m - 1)
 
     def halo_copies():
         right = lax.rem(me + 1, n)
@@ -105,12 +115,17 @@
         return pl.ds(pl.multiple_of(t * LANES, LANES), LANES)
 
     def short(g, t, start, count):
-        cols = columns(t)
+        cols = slice(t * LANES, (t + 1) * LANES) if isinstance(t, int) else columns(t)
         total = None
         for j in range(taps_n):
             term = taps[g, j : j + 1, cols] * x[g, t, pl.ds(SUB + start - j, count), :]
             total = term if total is None else total + term
         return total
+
+    def tree(terms):
+        while len(terms) > 1:
+            terms = [a + b for a, b in zip(terms[::2], terms[1::2])] + terms[len(terms) // 2 * 2 :]
+        return terms[0]
 
     def rounded(a):
         return a.astype(jnp.bfloat16).astype(jnp.float32)
@@ -150,28 +165,32 @@
             for t in range(tiles):
                 x[g, t, pl.ds(0, SUB), :] = jnp.zeros((SUB, LANES), jnp.float32)
 
-    def body_b(t, _):
-        cols = columns(t)
+    for t in range(tiles):
+        cols = slice(t * LANES, (t + 1) * LANES)
         u = rounded(short(1, t, 0, SUB) * short(2, t, 0, SUB))
         kv[t, pl.ds(0, SUB), :] = u
         for i in range(modes):
             end_f[i : i + 1, cols] = jnp.sum(state[i, t] + state0[i, t] * u, axis=0, keepdims=True)
-        return 0
-
-    lax.fori_loop(0, tiles, body_b, 0)
     end_b[...] = end_f[...].astype(jnp.bfloat16)
+
+    mate = me + 1 - 2 * lax.rem(me, 2)
+    pairs_n = n // 2
+
+    mate_copy = pltpu.make_async_remote_copy(
+        src_ref=end_b, dst_ref=mate_b, send_sem=mate_sem.at[0], recv_sem=mate_sem.at[1],
+        device_id={"ctx": mate}, device_id_type=pl.DeviceIdType.MESH,
+    )
+    mate_copy.start()
 
     def end_copy(slot, target):
         return pltpu.make_async_remote_copy(
-            src_ref=end_b, dst_ref=ends.at[slot], send_sem=end_send.at[target], recv_sem=end_recv.at[slot],
-            device_id={"ctx": target}, device_id_type=pl.DeviceIdType.MESH,
+            src_ref=pair_b, dst_ref=ends.at[slot], send_sem=end_send.at[target], recv_sem=end_recv.at[slot],
+            device_id={"ctx": 2 * target + side}, device_id_type=pl.DeviceIdType.MESH,
         )
 
     def send_end(j, _):
-        end_copy(me, j).start()
-        return 0
-
-    lax.fori_loop(me + 1, n, send_end, 0)
+        end_copy(pair, j).start()
+        return 0
 
     loads[4].wait()
 
@@ -184,13 +203,17 @@
             c = res[i : i + 1, cols] * scale
             w.append(c * jnp.exp(-(r * sub) / length))
             tailw[i, t] = c * jnp.exp(-(r * (sub + 1.0)) / length)
-        for b in range(blocks):
-            total = w[0]
-            for i in range(1, modes):
-                total = total + w[i]
-            filt[t, pl.ds(b * SUB, SUB), :] = total
-            if b < blocks - 1:
+        for b in range(0, blocks, 2):
+            first = tree(w)
+            w = [w[i] * step[i] for i in range(modes)]
+            both = jnp.concatenate([first, tree(w)], 0)
+            if b < blocks - 2:
                 w = [w[i] * step[i] for i in range(modes)]
+            hi = both.astype(jnp.bfloat16)
+            lo = (both - hi.astype(jnp.float32)).astype(jnp.bfloat16)
+            filt[pl.ds(b * SUB, 2 * SUB), cols] = hi
+            filt[pl.ds(rows + b * SUB, 2 * SUB), cols] = hi
+            filt[pl.ds(2 * rows + b * SUB, 2 * SUB), cols] = lo
         return 0
 
     lax.fori_loop(0, tiles, body_c, 0)
@@ -198,25 +221,32 @@
     for i in range(5, len(loads)):
         loads[i].wait()
 
-    def body_d(p, _):
-        t0 = 2 * p
+    mate_copy.wait_recv()
+    other = mate_b[...].astype(jnp.float32)
+    early = jnp.where(side == 0, end_f[...], other)
+    late = jnp.where(side == 0, other, end_f[...])
+    pair_b[...] = (early * a128[...] + late).astype(jnp.bfloat16)
+    lax.fori_loop(pair + 1, pairs_n, send_end, 0)
+
+    width = 2 * LANES
+    groups = [slice(c, c + width) for c in range(0, channels, width)]
+    for c in groups:
+        t0 = c.start // LANES
         u = jnp.concatenate([kv[t0], kv[t0 + 1]], 1).astype(jnp.bfloat16)
-        f = jnp.concatenate([filt[t0], filt[t0 + 1]], 1)
-        f_hi = f.astype(jnp.bfloat16)
-        f_lo = (f - f_hi.astype(jnp.float32)).astype(jnp.bfloat16)
-        both = fwd[...]
-        us = dot(both, jnp.concatenate([u, u], 0))
-        fs = dot(both, jnp.concatenate([f_hi, f_hi], 0)) + dot(both[:, :rows], f_lo)
-        ur, ui, fr, fi = us[:rows], us[rows:], fs[:rows], fs[rows:]
-        prod = jnp.concatenate([ur * fr - ui * fi, ur * fi + ui * fr], 0)
-        p_hi = prod.astype(jnp.bfloat16)
-        p_lo = (prod - p_hi.astype(jnp.float32)).astype(jnp.bfloat16)
-        y = dot(inv_hi[...], p_hi) + dot(inv_lo[...], p_hi) + dot(inv_hi[...], p_lo)
+        spec_f[:, c] = dot(fwd[...], filt[:, c])
+        spec_u[:, c] = dot(fwd[:, : 2 * rows], jnp.concatenate([u, u], 0))
+    for c in groups:
+        ur, ui, fr, fi = spec_u[:rows, c], spec_u[rows:, c], spec_f[:rows, c], spec_f[rows:, c]
+        for at, part in ((0, ur * fr - ui * fi), (rows, ur * fi + ui * fr)):
+            hi = part.astype(jnp.bfloat16)
+            prod_hi[at : at + rows, c] = hi
+            prod_lo[at : at + rows, c] = (part - hi.astype(jnp.float32)).astype(jnp.bfloat16)
+    for c in groups:
+        t0 = c.start // LANES
+        y = dot(inv[...], prod_hi[:, c])
+        y = y[:rows] + y[rows:] + dot(inv[:rows], prod_lo[:, c])
         long[t0] = y[:, :LANES]
         long[t0 + 1] = y[:, LANES:]
-        return 0
-
-    lax.fori_loop(0, tiles // 2, body_d, 0)
 
     @pl.when(me > 0)
     def _():
@@ -235,9 +265,10 @@
 
     def gather(i, carry):
         end_copy(i, i).wait_recv()
-        return carry * a128[...] + ends[i].astype(jnp.float32)
-
-    end_f[...] = lax.fori_loop(0, me, gather, jnp.zeros((modes, channels), jnp.float32))
+        return carry * (a128[...] * a128[...]) + ends[i].astype(jnp.float32)
+
+    carry = lax.fori_loop(0, pair, gather, jnp.zeros((modes, channels), jnp.float32))
+    end_f[...] = jnp.where(side == 0, carry, carry * a128[...] + mate_b[...].astype(jnp.float32))
     squares[...] = jnp.zeros_like(squares)
 
     def body_e(t, _):
@@ -247,10 +278,7 @@
         direct = skip[:, cols]
         for b in range(blocks):
             here = pl.ds(b * SUB, SUB)
-            total = w[0]
-            for i in range(1, modes):
-                total = total + w[i]
-            y = rounded(long[t, here, :] + total)
+            y = rounded(long[t, here, :] + tree(w))
             g = gated[t, here, :] * (y + direct * kv[t, here, :])
             gated[t, here, :] = g
             squares[here, :] += g * g
@@ -260,10 +288,14 @@
 
     lax.fori_loop(0, tiles, body_e, 0)
 
-    ones = jnp.ones((SUB, LANES), jnp.float32)
+    def halves(a, axis):
+        hi = a.astype(jnp.bfloat16)
+        return jnp.concatenate([hi, (a - hi.astype(jnp.float32)).astype(jnp.bfloat16)], axis)
+
     mine = lax.dot_general(
-        ones, squares[...], (((1,), (1,)), ((), ())), precision=HIGHEST, preferred_element_type=jnp.float32
-    )
+        jnp.ones((2 * SUB, 2 * LANES), jnp.bfloat16), halves(squares[...], 1), (((1,), (1,)), ((), ())),
+        preferred_element_type=jnp.float32,
+    )[:SUB]
     sums[lane_rank] = mine
 
     def sum_copy(d, slot):
@@ -282,7 +314,7 @@
         total = total + sums[d]
     inverse = 1.0 / jnp.sqrt(total / (channels * m) + 1e-05)
     spread = lax.dot_general(
-        inverse, ones * (1.0 / SUB), (((0,), (0,)), ((), ())), precision=HIGHEST,
+        halves(inverse, 0), jnp.full((2 * SUB, LANES), 1.0 / SUB, jnp.bfloat16), (((0,), (0,)), ((), ())),
         preferred_element_type=jnp.float32,
     )
 
@@ -297,10 +329,11 @@
         second.wait_send()
 
     def finish(j, _):
-        end_copy(me, j).wait_send()
-        return 0
-
-    lax.fori_loop(me + 1, n, finish, 0)
+        end_copy(pair, j).wait_send()
+        return 0
+
+    lax.fori_loop(pair + 1, pairs_n, finish, 0)
+    mate_copy.wait_send()
     for d in range(1, m):
         sum_copy(d, lane_rank).wait_send()
 
@@ -313,7 +346,7 @@
         modes = rates.shape[1]
         tiles = channels // LANES
         f32, bf16 = jnp.float32, jnp.bfloat16
-        fwd, inv_hi, inv_lo = (jnp.asarray(a) for a in tables(rows))
+        fwd, inv = (jnp.asarray(a) for a in tables(rows))
         tile3 = pltpu.VMEM((tiles, rows, LANES), f32)
         modal = pltpu.VMEM((modes, tiles, SUB, LANES), f32)
         flat = pltpu.VMEM((modes, channels), f32)
@@ -321,33 +354,39 @@
         return pl.pallas_call(
             functools.partial(kernel, n, m, modes, short_taps.shape[1], rows, channels, rows * n),
             out_shape=jax.ShapeDtypeStruct((rows, channels), bf16),
-            in_specs=[pl.BlockSpec(memory_space=pltpu.HBM)] * 9,
+            in_specs=[pl.BlockSpec(memory_space=pltpu.HBM)] * 8,
             out_specs=pl.BlockSpec(memory_space=pltpu.VMEM),
             scratch_shapes=[
                 pltpu.VMEM((2, 16, channels), bf16),
                 pltpu.VMEM(projected.shape[1:2] + (rows, channels), bf16),
                 pltpu.VMEM(short_taps.shape, f32), flat, flat,
                 pltpu.VMEM((1, channels), f32), pltpu.VMEM((1, channels), f32),
-                pltpu.VMEM(fwd.shape, bf16), pltpu.VMEM(inv_hi.shape, bf16), pltpu.VMEM(inv_lo.shape, bf16),
-                dma((11,)),
+                pltpu.VMEM(fwd.shape, bf16), pltpu.VMEM(inv.shape, bf16),
+                dma((10,)),
                 pltpu.VMEM((3, tiles, rows + SUB, LANES), f32),
-                tile3, modal, modal, tile3, modal, flat, flat, tile3, tile3,
+                tile3, modal, modal,
+                pltpu.VMEM((3 * rows, channels), bf16),
+                pltpu.VMEM((2 * rows, channels), f32), pltpu.VMEM((2 * rows, channels), f32),
+                pltpu.VMEM((2 * rows, channels), bf16), pltpu.VMEM((2 * rows, channels), bf16),
+                modal, flat, flat, tile3, tile3,
                 pltpu.VMEM((rows, LANES), f32),
                 pltpu.VMEM((16, channels), bf16),
                 pltpu.VMEM((16, channels), bf16),
                 pltpu.VMEM((16, channels), bf16),
                 flat,
                 pltpu.VMEM((modes, channels), bf16),
-                pltpu.VMEM((n, modes, channels), bf16),
+                pltpu.VMEM((modes, channels), bf16),
+                pltpu.VMEM((modes, channels), bf16),
+                pltpu.VMEM((n // 2, modes, channels), bf16),
                 pltpu.VMEM((m, SUB, LANES), f32),
-                dma((2,)), dma((2,)), dma((n,)), dma((n,)), dma((m,)), dma((m,)),
+                dma((2,)), dma((2,)), dma((n // 2,)), dma((n // 2,)), dma((m,)), dma((m,)), dma((2,)),
             ],
             compiler_params=pltpu.CompilerParams(
                 collective_id=0, has_side_effects=True, vmem_limit_bytes=60 * 1024 * 1024
             ),
         )(
             jnp.transpose(projected, (1, 0, 2)), short_taps, residues.T, rates.T,
-            skip_gain[None, :], norm_gain[None, :], fwd, inv_hi, inv_lo,
+            skip_gain[None, :], norm_gain[None, :], fwd, inv,
         )
 
     return jax.shard_map(

time: 20.5 us -> 19.9 us (0.971); the launches traced: 20.1 us -> 19.8 us
  Pallas kernels: 18.5 us -> 18.1 us
    pallas_call x1, Pallas kernels: 18.5 us -> 18.1 us  [shards(): pl.pallas_call(functools.partial(kernel, n, m, modes, short_taps.shape[1]...]
where the time goes in v2:
time: 19.9 us; the launch traced here: 19.8 us
  Pallas kernels  18.1 us (91%)
  local copies, waits for them, and re-layouts  1.67 us (8%)
    pallas_call x1, Pallas kernels, shards(): pl.pallas_call(functools.partial(kernel, n, m, modes, short_taps.shape[1]...  18.1 us
    unnamed x1, local copies, waits for them, and re-layouts  1.67 us

profile of v2, /device:TPU:25, one launch (start us, length us, event | category | flops | bytes accessed | tf_op | source)
XLA Modules:
  0.0 19.8 jit_solution(13516340379678765494)
XLA Ops:
  0.0 18.1 %shard_map.82 = bf16[128,1024]{1,0:T(8,128)(2,1)} custom-call(bf16[3,128,1024]{2,1,0:T(8,128)(2,1)} %bitcast.5, f32[3,7,1024]{2,1,0:T(8,128)} %taps_h.1, f32[16,1024]{1,0:T(8,128)} %bitcast.6, f32[16,1024]{1,0:T(8,128)} %bitcast.7, f32[1,1024]{1,0:T(1,128)} %bitcast.8, f32[1,1024]{1,0:T(1,128)} %bitcast.9, bf16[256,384]{1,0:T(8,128)(2,1)} %constant.4.clone.fwd_h, ...), custom_call_target="tpu_custom_call" | custom-call | tf_op jit(solution)/shard_map/pallas_call | solution.py:354
  18.1 1.7 %copy.10 = bf16[128,1024]{1,0:T(8,128)(2,1)} copy(bf16[128,1024]{1,0:T(8,128)(2,1)} %shard_map.82) | data formatting | bytes 524288

commit v3 on v2

--- a/solution.py
+++ b/solution.py
@@ -35,7 +35,7 @@
     proj_h, taps_h, res_h, rates_h, skip_h, gain_h, fwd_h, inv_h,
     out,
     rim, proj, taps, res, rates, skip, gain, fwd, inv, load_sem,
-    x, kv, state, state0, filt, spec_f, spec_u, prod_hi, prod_lo, tailw, a8, a128, long, gated, squares,
+    a1, a120, x, kv, state, state0, filt, spec_f, spec_u, prod_hi, prod_lo, tailw, a8, a128, long, gated, squares,
     send_kv, halo_kv, halo_q, end_f, end_b, mate_b, pair_b, ends, sums,
     halo_send, halo_recv, end_send, end_recv, sum_send, sum_recv, mate_sem,
 ):
@@ -47,8 +47,8 @@
 
     pairs = [
         (proj_h.at[pl.ds(1, 2), pl.ds(rows - 16, 16)], rim),
+        (rates_h, rates), (res_h, res), (taps_h, taps),
         (proj_h.at[pl.ds(1, 2)], proj.at[pl.ds(1, 2)]),
-        (taps_h, taps), (rates_h, rates), (res_h, res),
         (proj_h.at[0], proj.at[0]),
         (fwd_h, fwd), (inv_h, inv), (skip_h, skip), (gain_h, gain),
     ]
@@ -83,44 +83,8 @@
     rim_k = rim[0].astype(jnp.float32)[SUB:]
     rim_v = rim[1].astype(jnp.float32)[SUB:]
     send_kv[...] = jnp.concatenate([rim_k, rim_v], 0).astype(jnp.bfloat16)
-    pl.semaphore_wait(barrier, jnp.where(me < n - 1, 1, 0) + 1 + (n // 2 - 1 - pair) + m - 1)
-
-    def halo_copies():
-        right = lax.rem(me + 1, n)
-        first = pltpu.make_async_remote_copy(
-            src_ref=send_kv, dst_ref=halo_kv, send_sem=halo_send.at[0], recv_sem=halo_recv.at[0],
-            device_id={"ctx": right}, device_id_type=pl.DeviceIdType.MESH,
-        )
-        second = pltpu.make_async_remote_copy(
-            src_ref=proj_h.at[0, pl.ds(rows - 16, 16)], dst_ref=halo_q, send_sem=halo_send.at[1],
-            recv_sem=halo_recv.at[1], device_id={"ctx": right}, device_id_type=pl.DeviceIdType.MESH,
-        )
-        return first, second
-
-    @pl.when(me < n - 1)
-    def _():
-        first, second = halo_copies()
-        first.start()
-        second.start()
-
-    sub = lax.broadcasted_iota(jnp.int32, (SUB, LANES), 0).astype(jnp.float32)
-    scale = 1.0 / math.sqrt(length)
-    for i in (1, 2, 3):
-        loads[i].wait()
-    rate_all = rates[...]
-    a8[...] = jnp.exp(-(rate_all * SUB) / length)
-    a128[...] = jnp.exp(-(rate_all * rows) / length)
-
     def columns(t):
         return pl.ds(pl.multiple_of(t * LANES, LANES), LANES)
-
-    def short(g, t, start, count):
-        cols = slice(t * LANES, (t + 1) * LANES) if isinstance(t, int) else columns(t)
-        total = None
-        for j in range(taps_n):
-            term = taps[g, j : j + 1, cols] * x[g, t, pl.ds(SUB + start - j, count), :]
-            total = term if total is None else total + term
-        return total
 
     def tree(terms):
         while len(terms) > 1:
@@ -130,69 +94,15 @@
     def rounded(a):
         return a.astype(jnp.bfloat16).astype(jnp.float32)
 
-    def body_a(t, _):
-        cols = columns(t)
-        for g in (1, 2):
-            x[g, t, pl.ds(SUB, rows), :] = proj[g, :, cols].astype(jnp.float32)
-        kv[t, pl.ds(SUB, rows - SUB), :] = rounded(
-            short(1, t, SUB, rows - SUB) * short(2, t, SUB, rows - SUB)
-        )
-        step = [jnp.broadcast_to(a8[i : i + 1, cols], (SUB, LANES)) for i in range(modes)]
-        s = [kv[t, pl.ds(SUB, SUB), :]] * modes
-        for b in range(2, blocks):
-            u = kv[t, pl.ds(b * SUB, SUB), :]
-            s = [step[i] * s[i] + u for i in range(modes)]
-        for i in range(modes):
-            r = rates[i : i + 1, cols]
-            state[i, t] = s[i] * jnp.exp(-(r * (SUB - 1 - sub)) / length)
-            state0[i, t] = jnp.exp(-(r * (rows - 1 - sub)) / length)
-        return 0
-
-    lax.fori_loop(0, tiles, body_a, 0)
-
-    @pl.when(me > 0)
-    def _():
-        first, _second = halo_copies()
-        first.wait_recv()
-        tail = halo_kv[...].astype(jnp.float32)
-        for t in range(tiles):
-            x[1, t, pl.ds(0, SUB), :] = tail[:SUB, t * LANES : (t + 1) * LANES]
-            x[2, t, pl.ds(0, SUB), :] = tail[SUB:, t * LANES : (t + 1) * LANES]
-
-    @pl.when(me == 0)
-    def _():
-        for g in range(3):
-            for t in range(tiles):
-                x[g, t, pl.ds(0, SUB), :] = jnp.zeros((SUB, LANES), jnp.float32)
-
-    for t in range(tiles):
-        cols = slice(t * LANES, (t + 1) * LANES)
-        u = rounded(short(1, t, 0, SUB) * short(2, t, 0, SUB))
-        kv[t, pl.ds(0, SUB), :] = u
-        for i in range(modes):
-            end_f[i : i + 1, cols] = jnp.sum(state[i, t] + state0[i, t] * u, axis=0, keepdims=True)
-    end_b[...] = end_f[...].astype(jnp.bfloat16)
-
-    mate = me + 1 - 2 * lax.rem(me, 2)
-    pairs_n = n // 2
-
-    mate_copy = pltpu.make_async_remote_copy(
-        src_ref=end_b, dst_ref=mate_b, send_sem=mate_sem.at[0], recv_sem=mate_sem.at[1],
-        device_id={"ctx": mate}, device_id_type=pl.DeviceIdType.MESH,
-    )
-    mate_copy.start()
-
-    def end_copy(slot, target):
-        return pltpu.make_async_remote_copy(
-            src_ref=pair_b, dst_ref=ends.at[slot], send_sem=end_send.at[target], recv_sem=end_recv.at[slot],
-            device_id={"ctx": 2 * target + side}, device_id_type=pl.DeviceIdType.MESH,
-        )
-
-    def send_end(j, _):
-        end_copy(pair, j).start()
-        return 0
-
-    loads[4].wait()
+    sub = lax.broadcasted_iota(jnp.int32, (SUB, LANES), 0).astype(jnp.float32)
+    scale = 1.0 / math.sqrt(length)
+    for i in (1, 2):
+        loads[i].wait()
+    rate_all = rates[...]
+    a1[...] = jnp.exp(-rate_all / length)
+    a8[...] = jnp.exp(-(rate_all * SUB) / length)
+    a120[...] = jnp.exp(-(rate_all * (rows - SUB)) / length)
+    a128[...] = jnp.exp(-(rate_all * rows) / length)
 
     def body_c(t, _):
         cols = columns(t)
@@ -200,9 +110,12 @@
         w = []
         for i in range(modes):
             r = rates[i : i + 1, cols]
-            c = res[i : i + 1, cols] * scale
-            w.append(c * jnp.exp(-(r * sub) / length))
-            tailw[i, t] = c * jnp.exp(-(r * (sub + 1.0)) / length)
+            rest = jnp.exp(-(r * (SUB - 1 - sub)) / length)
+            state[i, t] = rest
+            state0[i, t] = rest * a120[i : i + 1, cols]
+            here = (res[i : i + 1, cols] * scale) * jnp.exp(-(r * sub) / length)
+            w.append(here)
+            tailw[i, t] = here * a1[i : i + 1, cols]
         for b in range(0, blocks, 2):
             first = tree(w)
             w = [w[i] * step[i] for i in range(modes)]
@@ -217,16 +130,98 @@
         return 0
 
     lax.fori_loop(0, tiles, body_c, 0)
+    pl.semaphore_wait(barrier, jnp.where(me < n - 1, 1, 0) + 1 + (n // 2 - 1 - pair) + m - 1)
+
+    def halo_copies():
+        right = lax.rem(me + 1, n)
+        first = pltpu.make_async_remote_copy(
+            src_ref=send_kv, dst_ref=halo_kv, send_sem=halo_send.at[0], recv_sem=halo_recv.at[0],
+            device_id={"ctx": right}, device_id_type=pl.DeviceIdType.MESH,
+        )
+        second = pltpu.make_async_remote_copy(
+            src_ref=proj_h.at[0, pl.ds(rows - 16, 16)], dst_ref=halo_q, send_sem=halo_send.at[1],
+            recv_sem=halo_recv.at[1], device_id={"ctx": right}, device_id_type=pl.DeviceIdType.MESH,
+        )
+        return first, second
+
+    @pl.when(me < n - 1)
+    def _():
+        first, second = halo_copies()
+        first.start()
+        second.start()
+
+    def short(g, t, start, count):
+        cols = slice(t * LANES, (t + 1) * LANES) if isinstance(t, int) else columns(t)
+        total = None
+        for j in range(taps_n):
+            term = taps[g, j : j + 1, cols] * x[g, t, pl.ds(SUB + start - j, count), :]
+            total = term if total is None else total + term
+        return total
+
+    def body_a(t, _):
+        cols = columns(t)
+        for g in (1, 2):
+            x[g, t, pl.ds(SUB, rows), :] = proj[g, :, cols].astype(jnp.float32)
+        kv[t, pl.ds(SUB, rows - SUB), :] = rounded(
+            short(1, t, SUB, rows - SUB) * short(2, t, SUB, rows - SUB)
+        )
+        step = [jnp.broadcast_to(a8[i : i + 1, cols], (SUB, LANES)) for i in range(modes)]
+        s = [kv[t, pl.ds(SUB, SUB), :]] * modes
+        for b in range(2, blocks):
+            u = kv[t, pl.ds(b * SUB, SUB), :]
+            s = [step[i] * s[i] + u for i in range(modes)]
+        for i in range(modes):
+            state[i, t] = s[i] * state[i, t]
+        return 0
+
+    for i in (3, 4):
+        loads[i].wait()
+    lax.fori_loop(0, tiles, body_a, 0)
+
+    @pl.when(me > 0)
+    def _():
+        first, _second = halo_copies()
+        first.wait_recv()
+        tail = halo_kv[...].astype(jnp.float32)
+        for t in range(tiles):
+            x[1, t, pl.ds(0, SUB), :] = tail[:SUB, t * LANES : (t + 1) * LANES]
+            x[2, t, pl.ds(0, SUB), :] = tail[SUB:, t * LANES : (t + 1) * LANES]
+
+    @pl.when(me == 0)
+    def _():
+        for g in range(3):
+            for t in range(tiles):
+                x[g, t, pl.ds(0, SUB), :] = jnp.zeros((SUB, LANES), jnp.float32)
+
+    for t in range(tiles):
+        cols = slice(t * LANES, (t + 1) * LANES)
+        u = rounded(short(1, t, 0, SUB) * short(2, t, 0, SUB))
+        kv[t, pl.ds(0, SUB), :] = u
+        for i in range(modes):
+            end_f[i : i + 1, cols] = jnp.sum(state[i, t] + state0[i, t] * u, axis=0, keepdims=True)
+    end_b[...] = end_f[...].astype(jnp.bfloat16)
+
+    mate = me + 1 - 2 * lax.rem(me, 2)
+    pairs_n = n // 2
+
+    mate_copy = pltpu.make_async_remote_copy(
+        src_ref=end_b, dst_ref=mate_b, send_sem=mate_sem.at[0], recv_sem=mate_sem.at[1],
+        device_id={"ctx": mate}, device_id_type=pl.DeviceIdType.MESH,
+    )
+    mate_copy.start()
+
+    def end_copy(slot, target):
+        return pltpu.make_async_remote_copy(
+            src_ref=pair_b, dst_ref=ends.at[slot], send_sem=end_send.at[target], recv_sem=end_recv.at[slot],
+            device_id={"ctx": 2 * target + side}, device_id_type=pl.DeviceIdType.MESH,
+        )
+
+    def send_end(j, _):
+        end_copy(pair, j).start()
+        return 0
 
     for i in range(5, len(loads)):
         loads[i].wait()
-
-    mate_copy.wait_recv()
-    other = mate_b[...].astype(jnp.float32)
-    early = jnp.where(side == 0, end_f[...], other)
-    late = jnp.where(side == 0, other, end_f[...])
-    pair_b[...] = (early * a128[...] + late).astype(jnp.bfloat16)
-    lax.fori_loop(pair + 1, pairs_n, send_end, 0)
 
     width = 2 * LANES
     groups = [slice(c, c + width) for c in range(0, channels, width)]
@@ -235,6 +230,13 @@
         u = jnp.concatenate([kv[t0], kv[t0 + 1]], 1).astype(jnp.bfloat16)
         spec_f[:, c] = dot(fwd[...], filt[:, c])
         spec_u[:, c] = dot(fwd[:, : 2 * rows], jnp.concatenate([u, u], 0))
+    mate_copy.wait_recv()
+    other = mate_b[...].astype(jnp.float32)
+    early = jnp.where(side == 0, end_f[...], other)
+    late = jnp.where(side == 0, other, end_f[...])
+    pair_b[...] = (early * a128[...] + late).astype(jnp.bfloat16)
+    lax.fori_loop(pair + 1, pairs_n, send_end, 0)
+
     for c in groups:
         ur, ui, fr, fi = spec_u[:rows, c], spec_u[rows:, c], spec_f[:rows, c], spec_f[rows:, c]
         for at, part in ((0, ur * fr - ui * fi), (rows, ur * fi + ui * fr)):
@@ -363,6 +365,7 @@
                 pltpu.VMEM((1, channels), f32), pltpu.VMEM((1, channels), f32),
                 pltpu.VMEM(fwd.shape, bf16), pltpu.VMEM(inv.shape, bf16),
                 dma((10,)),
+                flat, flat,
                 pltpu.VMEM((3, tiles, rows + SUB, LANES), f32),
                 tile3, modal, modal,
                 pltpu.VMEM((3 * rows, channels), bf16),
@@ -382,12 +385,15 @@
                 dma((2,)), dma((2,)), dma((n // 2,)), dma((n // 2,)), dma((m,)), dma((m,)), dma((2,)),
             ],
             compiler_params=pltpu.CompilerParams(
-                collective_id=0, has_side_effects=True, vmem_limit_bytes=60 * 1024 * 1024
+                collective_id=0, has_side_effects=True, vmem_limit_bytes=32 * 1024 * 1024
             ),
-        )(
-            jnp.transpose(projected, (1, 0, 2)), short_taps, residues.T, rates.T,
-            skip_gain[None, :], norm_gain[None, :], fwd, inv,
-        )
+        )(*(
+            pltpu.with_memory_space_constraint(a, pltpu.HBM)
+            for a in (
+                jnp.transpose(projected, (1, 0, 2)), short_taps, residues.T, rates.T,
+                skip_gain[None, :], norm_gain[None, :], fwd, inv,
+            )
+        ))
 
     return jax.shard_map(
         shards,

time: 19.9 us -> 18.3 us (0.920)
  local copies, waits for them, and re-layouts: 1.67 us -> 0.71 us
  Pallas kernels: 18.1 us -> 17.5 us
    unnamed x1, local copies, waits for them, and re-layouts: 1.67 us -> 0.71 us
    pallas_call x1, Pallas kernels: 18.1 us -> 17.5 us  [shards(): pl.pallas_call(functools.partial(kernel, n, m, modes, short_taps.shape[1]...]
where the time goes in v3:
time: 18.3 us; the launch traced here: 18.2 us
  Pallas kernels  17.5 us (96%)
  local copies, waits for them, and re-layouts  0.71 us (4%)
    pallas_call x1, Pallas kernels, shards(): pl.pallas_call(functools.partial(kernel, n, m, modes, short_taps.shape[1]...  17.5 us
    unnamed x1, local copies, waits for them, and re-layouts  0.71 us

profile of v3, /device:TPU:25, one launch (start us, length us, event | category | flops | bytes accessed | tf_op | source)
XLA Modules:
  0.0 18.2 jit_solution(10944420561804982147)
XLA Ops:
  0.0 17.5 %shard_map.82 = bf16[128,1024]{1,0:T(8,128)(2,1)S(1)} custom-call(bf16[3,128,1024]{2,1,0:T(8,128)(2,1)} %bitcast.5, f32[3,7,1024]{2,1,0:T(8,128)} %taps_h.1, f32[16,1024]{1,0:T(8,128)} %bitcast.6, f32[16,1024]{1,0:T(8,128)} %bitcast.7, f32[1,1024]{1,0:T(1,128)} %bitcast.8, f32[1,1024]{1,0:T(1,128)} %bitcast.9, bf16[256,384]{1,0:T(8,128)(2,1)} %constant.4.clone.fwd_h, ...), custom_call_target="tpu_custom_call" | custom-call | tf_op jit(solution)/shard_map/pallas_call | solution.py:356
  17.5 0.7 %copy.10 = bf16[128,1024]{1,0:T(8,128)(2,1)} copy(bf16[128,1024]{1,0:T(8,128)(2,1)S(1)} %shard_map.82) | data formatting | bytes 524288

commit v4 on v3

--- a/solution.py
+++ b/solution.py
@@ -94,7 +94,8 @@
     def rounded(a):
         return a.astype(jnp.bfloat16).astype(jnp.float32)
 
-    sub = lax.broadcasted_iota(jnp.int32, (SUB, LANES), 0).astype(jnp.float32)
+    sub = lax.broadcasted_iota(jnp.int32, (SUB, LANES), 0)
+    odd, second, third = (sub & 1) > 0, (sub & 2) > 0, (sub & 4) > 0
     scale = 1.0 / math.sqrt(length)
     for i in (1, 2):
         loads[i].wait()
@@ -109,13 +110,16 @@
         step = [jnp.broadcast_to(a8[i : i + 1, cols], (SUB, LANES)) for i in range(modes)]
         w = []
         for i in range(modes):
-            r = rates[i : i + 1, cols]
-            rest = jnp.exp(-(r * (SUB - 1 - sub)) / length)
+            one = a1[i : i + 1, cols]
+            two = one * one
+            four = two * two
+            rest = jnp.where(odd, 1.0, one) * jnp.where(second, 1.0, two) * jnp.where(third, 1.0, four)
+            past = jnp.where(odd, one, 1.0) * jnp.where(second, two, 1.0) * jnp.where(third, four, 1.0)
             state[i, t] = rest
             state0[i, t] = rest * a120[i : i + 1, cols]
-            here = (res[i : i + 1, cols] * scale) * jnp.exp(-(r * sub) / length)
+            here = (res[i : i + 1, cols] * scale) * past
             w.append(here)
-            tailw[i, t] = here * a1[i : i + 1, cols]
+            tailw[i, t] = here * one
         for b in range(0, blocks, 2):
             first = tree(w)
             w = [w[i] * step[i] for i in range(modes)]
@@ -263,7 +267,7 @@
         gated[t] = short(0, t, 0, rows)
         return 0
 
-    lax.fori_loop(0, tiles, body_q, 0)
+    lax.fori_loop(0, tiles, body_q, 0, unroll=2)
 
     def gather(i, carry):
         end_copy(i, i).wait_recv()

time: 18.3 us -> 18.3 us (level)
  no operation moved by 1% of the time
where the time goes in v4:
time: 18.3 us; the launch traced here: 18.2 us
  Pallas kernels  17.5 us (96%)
  local copies, waits for them, and re-layouts  0.71 us (4%)
    pallas_call x1, Pallas kernels, shards(): pl.pallas_call(functools.partial(kernel, n, m, modes, short_taps.shape[1]...  17.5 us
    unnamed x1, local copies, waits for them, and re-layouts  0.71 us

profile of v4, /device:TPU:25, one launch (start us, length us, event | category | flops | bytes accessed | tf_op | source)
XLA Modules:
  0.0 18.2 jit_solution(17454852604529907523)
XLA Ops:
  0.0 17.5 %shard_map.82 = bf16[128,1024]{1,0:T(8,128)(2,1)S(1)} custom-call(bf16[3,128,1024]{2,1,0:T(8,128)(2,1)} %bitcast.5, f32[3,7,1024]{2,1,0:T(8,128)} %taps_h.1, f32[16,1024]{1,0:T(8,128)} %bitcast.6, f32[16,1024]{1,0:T(8,128)} %bitcast.7, f32[1,1024]{1,0:T(1,128)} %bitcast.8, f32[1,1024]{1,0:T(1,128)} %bitcast.9, bf16[256,384]{1,0:T(8,128)(2,1)} %constant.4.clone.fwd_h, ...), custom_call_target="tpu_custom_call" | custom-call | tf_op jit(solution)/shard_map/pallas_call | solution.py:360
  17.5 0.7 %copy.10 = bf16[128,1024]{1,0:T(8,128)(2,1)} copy(bf16[128,1024]{1,0:T(8,128)(2,1)S(1)} %shard_map.82) | data formatting | bytes 524288

commit v5 on v3

--- a/solution.py
+++ b/solution.py
@@ -18,6 +18,8 @@
     freq = (np.arange(rows) + 0.5)[:, None] * (2.0 * math.pi / (2 * rows))
     angle = freq * np.arange(rows)[None, :]
     forward = np.concatenate([np.cos(angle), -np.sin(angle)], 0)
+    order = np.arange(rows).reshape(SUB, rows // SUB).T.reshape(-1)
+    forward = forward[:, order]
     inverse = forward.T / rows
 
     def pair(a):
@@ -35,7 +37,7 @@
     proj_h, taps_h, res_h, rates_h, skip_h, gain_h, fwd_h, inv_h,
     out,
     rim, proj, taps, res, rates, skip, gain, fwd, inv, load_sem,
-    a1, a120, x, kv, state, state0, filt, spec_f, spec_u, prod_hi, prod_lo, tailw, a8, a128, long, gated, squares,
+    a1, a16, x, kv, state, filt, spec_f, spec_u, prod_hi, prod_lo, tailw, a128, long, gated, squares,
     send_kv, halo_kv, halo_q, end_f, end_b, mate_b, pair_b, ends, sums,
     halo_send, halo_recv, end_send, end_recv, sum_send, sum_recv, mate_sem,
 ):
@@ -83,6 +85,26 @@
     rim_k = rim[0].astype(jnp.float32)[SUB:]
     rim_v = rim[1].astype(jnp.float32)[SUB:]
     send_kv[...] = jnp.concatenate([rim_k, rim_v], 0).astype(jnp.bfloat16)
+    pl.semaphore_wait(barrier, jnp.where(me < n - 1, 1, 0) + 1 + (n // 2 - 1 - pair) + m - 1)
+
+    def halo_copies():
+        right = lax.rem(me + 1, n)
+        first = pltpu.make_async_remote_copy(
+            src_ref=send_kv, dst_ref=halo_kv, send_sem=halo_send.at[0], recv_sem=halo_recv.at[0],
+            device_id={"ctx": right}, device_id_type=pl.DeviceIdType.MESH,
+        )
+        second = pltpu.make_async_remote_copy(
+            src_ref=proj_h.at[0, pl.ds(rows - 16, 16)], dst_ref=halo_q, send_sem=halo_send.at[1],
+            recv_sem=halo_recv.at[1], device_id={"ctx": right}, device_id_type=pl.DeviceIdType.MESH,
+        )
+        return first, second
+
+    @pl.when(me < n - 1)
+    def _():
+        first, second = halo_copies()
+        first.start()
+        second.start()
+
     def columns(t):
         return pl.ds(pl.multiple_of(t * LANES, LANES), LANES)
 
@@ -94,26 +116,28 @@
     def rounded(a):
         return a.astype(jnp.bfloat16).astype(jnp.float32)
 
-    sub = lax.broadcasted_iota(jnp.int32, (SUB, LANES), 0).astype(jnp.float32)
+    sub = lax.broadcasted_iota(jnp.int32, (SUB, LANES), 0)
+    odd, second, third = (sub & 1) > 0, (sub & 2) > 0, (sub & 4) > 0
     scale = 1.0 / math.sqrt(length)
     for i in (1, 2):
         loads[i].wait()
     rate_all = rates[...]
     a1[...] = jnp.exp(-rate_all / length)
-    a8[...] = jnp.exp(-(rate_all * SUB) / length)
-    a120[...] = jnp.exp(-(rate_all * (rows - SUB)) / length)
+    a16[...] = jnp.exp(-(rate_all * blocks) / length)
     a128[...] = jnp.exp(-(rate_all * rows) / length)
 
     def body_c(t, _):
         cols = columns(t)
-        step = [jnp.broadcast_to(a8[i : i + 1, cols], (SUB, LANES)) for i in range(modes)]
+        step = [jnp.broadcast_to(a1[i : i + 1, cols], (SUB, LANES)) for i in range(modes)]
         w = []
         for i in range(modes):
-            r = rates[i : i + 1, cols]
-            rest = jnp.exp(-(r * (SUB - 1 - sub)) / length)
+            one = a16[i : i + 1, cols]
+            two = one * one
+            four = two * two
+            rest = jnp.where(odd, 1.0, one) * jnp.where(second, 1.0, two) * jnp.where(third, 1.0, four)
+            past = jnp.where(odd, one, 1.0) * jnp.where(second, two, 1.0) * jnp.where(third, four, 1.0)
             state[i, t] = rest
-            state0[i, t] = rest * a120[i : i + 1, cols]
-            here = (res[i : i + 1, cols] * scale) * jnp.exp(-(r * sub) / length)
+            here = (res[i : i + 1, cols] * scale) * past
             w.append(here)
             tailw[i, t] = here * a1[i : i + 1, cols]
         for b in range(0, blocks, 2):
@@ -130,54 +154,30 @@
         return 0
 
     lax.fori_loop(0, tiles, body_c, 0)
-    pl.semaphore_wait(barrier, jnp.where(me < n - 1, 1, 0) + 1 + (n // 2 - 1 - pair) + m - 1)
-
-    def halo_copies():
-        right = lax.rem(me + 1, n)
-        first = pltpu.make_async_remote_copy(
-            src_ref=send_kv, dst_ref=halo_kv, send_sem=halo_send.at[0], recv_sem=halo_recv.at[0],
-            device_id={"ctx": right}, device_id_type=pl.DeviceIdType.MESH,
-        )
-        second = pltpu.make_async_remote_copy(
-            src_ref=proj_h.at[0, pl.ds(rows - 16, 16)], dst_ref=halo_q, send_sem=halo_send.at[1],
-            recv_sem=halo_recv.at[1], device_id={"ctx": right}, device_id_type=pl.DeviceIdType.MESH,
-        )
-        return first, second
-
-    @pl.when(me < n - 1)
-    def _():
-        first, second = halo_copies()
-        first.start()
-        second.start()
-
-    def short(g, t, start, count):
-        cols = slice(t * LANES, (t + 1) * LANES) if isinstance(t, int) else columns(t)
-        total = None
-        for j in range(taps_n):
-            term = taps[g, j : j + 1, cols] * x[g, t, pl.ds(SUB + start - j, count), :]
-            total = term if total is None else total + term
-        return total
+    def short(g, t):
+        cols = columns(t)
+        tap = [jnp.broadcast_to(taps[g, j : j + 1, cols], (SUB, LANES)) for j in range(taps_n)]
+        x[g, t, pl.ds(SUB, rows), :] = proj[g, :, cols].astype(jnp.float32)
+        shifted = {
+            k: x[g, t, pl.ds(SUB + k, SUB, stride=blocks), :] for k in range(1 - taps_n, blocks)
+        }
+        return [tree([tap[j] * shifted[k - j] for j in range(taps_n)]) for k in range(blocks)]
 
     def body_a(t, _):
         cols = columns(t)
-        for g in (1, 2):
-            x[g, t, pl.ds(SUB, rows), :] = proj[g, :, cols].astype(jnp.float32)
-        kv[t, pl.ds(SUB, rows - SUB), :] = rounded(
-            short(1, t, SUB, rows - SUB) * short(2, t, SUB, rows - SUB)
-        )
-        step = [jnp.broadcast_to(a8[i : i + 1, cols], (SUB, LANES)) for i in range(modes)]
-        s = [kv[t, pl.ds(SUB, SUB), :]] * modes
-        for b in range(2, blocks):
-            u = kv[t, pl.ds(b * SUB, SUB), :]
-            s = [step[i] * s[i] + u for i in range(modes)]
+        u = [rounded(a * b) for a, b in zip(short(1, t), short(2, t))]
+        step = [jnp.broadcast_to(a1[i : i + 1, cols], (SUB, LANES)) for i in range(modes)]
+        s = [u[0]] * modes
+        kv[t, pl.ds(0, SUB), :] = u[0]
+        for b in range(1, blocks):
+            kv[t, pl.ds(b * SUB, SUB), :] = u[b]
+            s = [step[i] * s[i] + u[b] for i in range(modes)]
         for i in range(modes):
-            state[i, t] = s[i] * state[i, t]
+            end_f[i : i + 1, cols] = jnp.sum(s[i] * state[i, t], axis=0, keepdims=True)
         return 0
 
     for i in (3, 4):
         loads[i].wait()
-    lax.fori_loop(0, tiles, body_a, 0)
-
     @pl.when(me > 0)
     def _():
         first, _second = halo_copies()
@@ -193,12 +193,7 @@
             for t in range(tiles):
                 x[g, t, pl.ds(0, SUB), :] = jnp.zeros((SUB, LANES), jnp.float32)
 
-    for t in range(tiles):
-        cols = slice(t * LANES, (t + 1) * LANES)
-        u = rounded(short(1, t, 0, SUB) * short(2, t, 0, SUB))
-        kv[t, pl.ds(0, SUB), :] = u
-        for i in range(modes):
-            end_f[i : i + 1, cols] = jnp.sum(state[i, t] + state0[i, t] * u, axis=0, keepdims=True)
+    lax.fori_loop(0, tiles, body_a, 0)
     end_b[...] = end_f[...].astype(jnp.bfloat16)
 
     mate = me + 1 - 2 * lax.rem(me, 2)
@@ -259,8 +254,7 @@
             x[0, t, pl.ds(0, SUB), :] = tail[:, t * LANES : (t + 1) * LANES]
 
     def body_q(t, _):
-        x[0, t, pl.ds(SUB, rows), :] = proj[0, :, columns(t)].astype(jnp.float32)
-        gated[t] = short(0, t, 0, rows)
+        gated[t] = jnp.concatenate(short(0, t), 0)
         return 0
 
     lax.fori_loop(0, tiles, body_q, 0)
@@ -275,7 +269,7 @@
 
     def body_e(t, _):
         cols = columns(t)
-        step = [jnp.broadcast_to(a8[i : i + 1, cols], (SUB, LANES)) for i in range(modes)]
+        step = [jnp.broadcast_to(a1[i : i + 1, cols], (SUB, LANES)) for i in range(modes)]
         w = [tailw[i, t] * end_f[i : i + 1, cols] for i in range(modes)]
         direct = skip[:, cols]
         for b in range(blocks):
@@ -322,7 +316,10 @@
 
     for t in range(tiles):
         cols = slice(t * LANES, (t + 1) * LANES)
-        out[:, cols] = (gated[t] * gain[:, cols] * spread).astype(jnp.bfloat16)
+        result = gated[t] * gain[:, cols] * spread
+        for k in range(blocks):
+            long[t, pl.ds(k, SUB, stride=blocks), :] = result[k * SUB : (k + 1) * SUB]
+        out[:, cols] = long[t].astype(jnp.bfloat16)
 
     @pl.when(me < n - 1)
     def _():
@@ -367,11 +364,11 @@
                 dma((10,)),
                 flat, flat,
                 pltpu.VMEM((3, tiles, rows + SUB, LANES), f32),
-                tile3, modal, modal,
+                tile3, modal,
                 pltpu.VMEM((3 * rows, channels), bf16),
                 pltpu.VMEM((2 * rows, channels), f32), pltpu.VMEM((2 * rows, channels), f32),
                 pltpu.VMEM((2 * rows, channels), bf16), pltpu.VMEM((2 * rows, channels), bf16),
-                modal, flat, flat, tile3, tile3,
+                modal, flat, tile3, tile3,
                 pltpu.VMEM((rows, LANES), f32),
                 pltpu.VMEM((16, channels), bf16),
                 pltpu.VMEM((16, channels), bf16),

time: 18.3 us -> 19.8 us (1.082)
  Pallas kernels: 17.5 us -> 19 us
    pallas_call x1, Pallas kernels: 17.5 us -> 19 us  [shards(): pl.pallas_call(functools.partial(kernel, n, m, modes, short_taps.shape[1]...]
where the time goes in v5:
time: 19.8 us; the launch traced here: 19.7 us
  Pallas kernels  19 us (96%)
  local copies, waits for them, and re-layouts  0.71 us (4%)
    pallas_call x1, Pallas kernels, shards(): pl.pallas_call(functools.partial(kernel, n, m, modes, short_taps.shape[1]...  19 us
    unnamed x1, local copies, waits for them, and re-layouts  0.71 us

profile of v5, /device:TPU:25, one launch (start us, length us, event | category | flops | bytes accessed | tf_op | source)
XLA Modules:
  0.0 19.7 jit_solution(18223599319519308250)
XLA Ops:
  0.0 19.0 %shard_map.82 = bf16[128,1024]{1,0:T(8,128)(2,1)S(1)} custom-call(bf16[3,128,1024]{2,1,0:T(8,128)(2,1)} %bitcast.5, f32[3,7,1024]{2,1,0:T(8,128)} %taps_h.1, f32[16,1024]{1,0:T(8,128)} %bitcast.6, f32[16,1024]{1,0:T(8,128)} %bitcast.7, f32[1,1024]{1,0:T(1,128)} %bitcast.8, f32[1,1024]{1,0:T(1,128)} %bitcast.9, bf16[256,384]{1,0:T(8,128)(2,1)} %constant.4.clone.fwd_h, ...), custom_call_target="tpu_custom_call" | custom-call | tf_op jit(solution)/shard_map/pallas_call | solution.py:353
  19.0 0.7 %copy.10 = bf16[128,1024]{1,0:T(8,128)(2,1)} copy(bf16[128,1024]{1,0:T(8,128)(2,1)S(1)} %shard_map.82) | data formatting | bytes 524288

commit v6 on v5

--- a/solution.py
+++ b/solution.py
@@ -85,26 +85,6 @@
     rim_k = rim[0].astype(jnp.float32)[SUB:]
     rim_v = rim[1].astype(jnp.float32)[SUB:]
     send_kv[...] = jnp.concatenate([rim_k, rim_v], 0).astype(jnp.bfloat16)
-    pl.semaphore_wait(barrier, jnp.where(me < n - 1, 1, 0) + 1 + (n // 2 - 1 - pair) + m - 1)
-
-    def halo_copies():
-        right = lax.rem(me + 1, n)
-        first = pltpu.make_async_remote_copy(
-            src_ref=send_kv, dst_ref=halo_kv, send_sem=halo_send.at[0], recv_sem=halo_recv.at[0],
-            device_id={"ctx": right}, device_id_type=pl.DeviceIdType.MESH,
-        )
-        second = pltpu.make_async_remote_copy(
-            src_ref=proj_h.at[0, pl.ds(rows - 16, 16)], dst_ref=halo_q, send_sem=halo_send.at[1],
-            recv_sem=halo_recv.at[1], device_id={"ctx": right}, device_id_type=pl.DeviceIdType.MESH,
-        )
-        return first, second
-
-    @pl.when(me < n - 1)
-    def _():
-        first, second = halo_copies()
-        first.start()
-        second.start()
-
     def columns(t):
         return pl.ds(pl.multiple_of(t * LANES, LANES), LANES)
 
@@ -154,6 +134,26 @@
         return 0
 
     lax.fori_loop(0, tiles, body_c, 0)
+    pl.semaphore_wait(barrier, jnp.where(me < n - 1, 1, 0) + 1 + (n // 2 - 1 - pair) + m - 1)
+
+    def halo_copies():
+        right = lax.rem(me + 1, n)
+        first = pltpu.make_async_remote_copy(
+            src_ref=send_kv, dst_ref=halo_kv, send_sem=halo_send.at[0], recv_sem=halo_recv.at[0],
+            device_id={"ctx": right}, device_id_type=pl.DeviceIdType.MESH,
+        )
+        second = pltpu.make_async_remote_copy(
+            src_ref=proj_h.at[0, pl.ds(rows - 16, 16)], dst_ref=halo_q, send_sem=halo_send.at[1],
+            recv_sem=halo_recv.at[1], device_id={"ctx": right}, device_id_type=pl.DeviceIdType.MESH,
+        )
+        return first, second
+
+    @pl.when(me < n - 1)
+    def _():
+        first, second = halo_copies()
+        first.start()
+        second.start()
+
     def short(g, t):
         cols = columns(t)
         tap = [jnp.broadcast_to(taps[g, j : j + 1, cols], (SUB, LANES)) for j in range(taps_n)]

time: 19.8 us -> 19.8 us (level)
  no operation moved by 1% of the time
where the time goes in v6:
time: 19.8 us; the launch traced here: 19.7 us
  Pallas kernels  19 us (96%)
  local copies, waits for them, and re-layouts  0.71 us (4%)
    pallas_call x1, Pallas kernels, shards(): pl.pallas_call(functools.partial(kernel, n, m, modes, short_taps.shape[1]...  19 us
    unnamed x1, local copies, waits for them, and re-layouts  0.71 us

profile of v6, /device:TPU:25, one launch (start us, length us, event | category | flops | bytes accessed | tf_op | source)
XLA Modules:
  0.0 19.7 jit_solution(459394222656005748)
XLA Ops:
  0.0 19.0 %shard_map.82 = bf16[128,1024]{1,0:T(8,128)(2,1)S(1)} custom-call(bf16[3,128,1024]{2,1,0:T(8,128)(2,1)} %bitcast.5, f32[3,7,1024]{2,1,0:T(8,128)} %taps_h.1, f32[16,1024]{1,0:T(8,128)} %bitcast.6, f32[16,1024]{1,0:T(8,128)} %bitcast.7, f32[1,1024]{1,0:T(1,128)} %bitcast.8, f32[1,1024]{1,0:T(1,128)} %bitcast.9, bf16[256,384]{1,0:T(8,128)(2,1)} %constant.4.clone.fwd_h, ...), custom_call_target="tpu_custom_call" | custom-call | tf_op jit(solution)/shard_map/pallas_call | solution.py:353
  19.0 0.7 %copy.10 = bf16[128,1024]{1,0:T(8,128)(2,1)} copy(bf16[128,1024]{1,0:T(8,128)(2,1)S(1)} %shard_map.82) | data formatting | bytes 524288

commit v7 on v3

--- a/solution.py
+++ b/solution.py
@@ -263,7 +263,7 @@
         gated[t] = short(0, t, 0, rows)
         return 0
 
-    lax.fori_loop(0, tiles, body_q, 0)
+    lax.fori_loop(0, tiles, body_q, 0, unroll=2)
 
     def gather(i, carry):
         end_copy(i, i).wait_recv()
@@ -288,7 +288,7 @@
                 w = [w[i] * step[i] for i in range(modes)]
         return 0
 
-    lax.fori_loop(0, tiles, body_e, 0)
+    lax.fori_loop(0, tiles, body_e, 0, unroll=2)
 
     def halves(a, axis):
         hi = a.astype(jnp.bfloat16)

time: 18.3 us -> 18.3 us (level)
  no operation moved by 1% of the time
where the time goes in v7:
time: 18.3 us; the launch traced here: 18.2 us
  Pallas kernels  17.4 us (95%)
  local copies, waits for them, and re-layouts  0.71 us (4%)
    pallas_call x1, Pallas kernels, shards(): pl.pallas_call(functools.partial(kernel, n, m, modes, short_taps.shape[1]...  17.4 us
    unnamed x1, local copies, waits for them, and re-layouts  0.71 us

profile of v7, /device:TPU:25, one launch (start us, length us, event | category | flops | bytes accessed | tf_op | source)
XLA Modules:
  0.0 18.2 jit_solution(14795788056806838301)
XLA Ops:
  0.0 17.4 %shard_map.82 = bf16[128,1024]{1,0:T(8,128)(2,1)S(1)} custom-call(bf16[3,128,1024]{2,1,0:T(8,128)(2,1)} %bitcast.5, f32[3,7,1024]{2,1,0:T(8,128)} %taps_h.1, f32[16,1024]{1,0:T(8,128)} %bitcast.6, f32[16,1024]{1,0:T(8,128)} %bitcast.7, f32[1,1024]{1,0:T(1,128)} %bitcast.8, f32[1,1024]{1,0:T(1,128)} %bitcast.9, bf16[256,384]{1,0:T(8,128)(2,1)} %constant.4.clone.fwd_h, ...), custom_call_target="tpu_custom_call" | custom-call | tf_op jit(solution)/shard_map/pallas_call | solution.py:356
  17.5 0.7 %copy.10 = bf16[128,1024]{1,0:T(8,128)(2,1)} copy(bf16[128,1024]{1,0:T(8,128)(2,1)S(1)} %shard_map.82) | data formatting | bytes 524288
